TPU v7x, 32 devices: a whole 2x2x4 slice. The times are simulated.
32 devices in a mesh: freq: 4 (over x, core), tile: 8 (over z, y).
Axes of the slice: x: 2, y: 2, z: 4, core: 2. Of those that a mesh axis runs over, the one named last changes fastest.
Arguments:
- virtual_source_trace: bfloat16 [128, 4, 8400], P(('freq', 'tile')), may hold values from -6 to 6
- v_bases: bfloat16 [4, 192, 120, 2, 32, 70], P('freq', 'tile'), may hold values from -0.75 to 0.75
- u_bases: bfloat16 [4, 192, 120, 2, 32, 70], P('freq', 'tile'), may hold values from -0.09375 to 0.09375
- ranks: int32 [4, 192, 120], P('freq', 'tile'), may hold values from 16 to 32, as said below
- freq_bin: int32 [4], replicated, may hold values from 1 to 63
- slab_order: int32 [32], replicated, may hold values from 0 to 31, each once
Outputs:
- redatumed: bfloat16 [128, 4, 13440], P(('freq', 'tile'))
Inputs may be any that keep to these rules, and one draw needn't show every extreme that they name: `ranks`: every rank is 16 or 32.
All inputs are finite; a program needn't handle non-finite values.
Results may differ from a plain program's by a relative error of at most 0.008.
Values may be sent and summed in bfloat16 or wider, within the bound.
No kernel may reach another device: no remote copies, remote signals or barrier semaphores. Data moves between devices by JAX's collectives and lax.ppermute only.
A program may use at most 192 MiB of HBM per device.

v0:
```python
import math

import jax
import jax.numpy as jnp
from jax import lax
from jax.sharding import PartitionSpec as P


def angles_of(freq_bin, times, total):
    products = freq_bin[:, None] * times[None, :] % total
    return products.astype(jnp.float32) * (2.0 * math.pi / total)


def apply_kernel(v_part, u_part, rank_part, frequency_spectra):
    width = v_part.shape[3]
    projected = jnp.einsum(
        "ijcrp,dvjp->ijcdrv", v_part, frequency_spectra, preferred_element_type=jnp.float32
    )
    coef_re = projected[:, :, 0, 0] - projected[:, :, 1, 1]
    coef_im = projected[:, :, 0, 1] + projected[:, :, 1, 0]
    rank_mask = (jnp.arange(width, dtype=jnp.int32)[None, None, :] < rank_part[:, :, None]).astype(
        jnp.float32
    )[..., None]
    coefs = jnp.stack([coef_re * rank_mask, coef_im * rank_mask], axis=2).astype(jnp.bfloat16)
    rows_dev = v_part.shape[0] * v_part.shape[4]
    expanded = jnp.einsum("ijcrq,ijdrm->cdmiq", u_part, coefs, preferred_element_type=jnp.float32)
    out_re = (expanded[0, 0] - expanded[1, 1]).reshape(coefs.shape[4], rows_dev)
    out_im = (expanded[0, 1] + expanded[1, 0]).reshape(coefs.shape[4], rows_dev)
    return jnp.stack([out_re, out_im])


def local(virtual_source_trace, v_bases, u_bases, ranks, freq_bin, slab_order):
    n_tile = lax.axis_size("tile")
    n_freq = lax.axis_size("freq")
    steps_dev = virtual_source_trace.shape[0]
    sources = virtual_source_trace.shape[1]
    total = steps_dev * n_freq * n_tile
    count_freq = freq_bin.shape[0]
    device = lax.axis_index("freq") * n_tile + lax.axis_index("tile")
    first = lax.dynamic_index_in_dim(slab_order, device, 0, keepdims=False) * steps_dev
    times = first + jnp.arange(steps_dev, dtype=jnp.int32)
    angles = angles_of(freq_bin, times, total)
    forward = jnp.stack([jnp.cos(angles), -jnp.sin(angles)], axis=1) / math.sqrt(total)
    signal = virtual_source_trace.astype(jnp.float32)
    partial_value = jnp.einsum("fct,tvs->fcvs", forward, signal, precision=lax.Precision.HIGHEST)
    grouped = lax.psum_scatter(partial_value, "freq", scatter_dimension=0, tiled=True)
    frequency_spectra = lax.psum(grouped, "tile").astype(jnp.bfloat16)
    columns = v_bases.shape[2]
    tile_width = v_bases.shape[5]
    frequency_spectra = frequency_spectra.reshape(2, sources, columns, tile_width)
    received = apply_kernel(v_bases[0], u_bases[0], ranks[0], frequency_spectra)
    piece = received[None]
    grouped_rows = lax.all_gather(piece, "tile", axis=0, tiled=True)
    gathered = lax.all_gather(grouped_rows.astype(jnp.bfloat16), "freq", axis=0, tiled=True).astype(
        grouped_rows.dtype
    )
    gathered = gathered.reshape(n_freq, n_tile, 2, sources, -1)
    inverse = jnp.stack([jnp.cos(angles.T), -jnp.sin(angles.T)], axis=2) / math.sqrt(count_freq)
    redatumed = jnp.einsum("tgc,gkcvn->tvkn", inverse, gathered, precision=lax.Precision.HIGHEST)
    return redatumed.reshape(steps_dev, sources, -1).astype(jnp.bfloat16)


def solution(mesh):
    in_specs = (
        P(("freq", "tile"), None, None),
        P("freq", "tile", None, None, None, None),
        P("freq", "tile", None, None, None, None),
        P("freq", "tile", None),
        P(),
        P(),
    )
    out_specs = P(("freq", "tile"), None, None)
    return jax.shard_map(local, mesh=mesh, in_specs=in_specs, out_specs=out_specs, check_vma=False)
```

profile of v0, /device:TPU:0, one launch (start us, length us, event | category | flops | bytes accessed | tf_op | source)
XLA Modules:
  0.0 292.9 jit_solution(8992207273104399960)
XLA Ops:
  6.5 0.0 all-reduce.4.cloned.1.call-start
  6.5 1.2 dynamic_slice.4
  8.4 0.8 fusion.37
  9.2 1.7 fusion.16
  10.9 1.3 copy.76
  12.2 0.0 all-reduce.4.cloned.1.call-update
  12.3 0.0 copy-start
  12.3 0.0 copy-start.2
  12.3 0.0 copy-start.1
  12.3 76.5 %copy.91 = bf16[24,120,2,32,70,1]{4,3,2,0,5,1:T(8,128)(2,1)} copy(bf16[24,120,2,32,70,1]{1,3,4,2,0,5:T(8,128)(2,1)} %bitcast.77) | data formatting | bytes 51609600 | tf_op jit(solution)/shard_map/squeeze | solution.py:51
  88.8 0.1 copy.81
  88.9 0.0 copy-done.2
  88.9 0.6 dynamic-slice
  89.5 0.0 copy-done.1
  89.5 0.1 fusion.36
  89.6 0.4 fusion.11
  90.1 0.0 all-reduce.4.cloned.1.call-done
  90.1 1.6 constant_dynamic-slice_fusion
  91.7 42.3 %all-reduce.5 = bf16[1,2,4,8400]{3,2,1,0:T(4,128)(2,1)S(1)} all-reduce(f32[1,2,4,8400]{3,2,1,0:T(4,128)S(1)} %constant_dynamic-slice_fusion), channel_id=1, replica_groups=mesh['freq'=4,'tile'=8] {'tile'}, use_global_device_ids=true, to_apply=%region_1.2 | all-reduce | flops 67200 | bytes 403200 | tf_op jit(solution)/shard_map/psum | solution.py:47
  134.1 0.3 reshape.343
  134.4 67.3 %convolution_bitcast_fusion = f32[24,120,2,2,32,4]{4,5,2,0,3,1:T(4,128)} fusion(bf16[24,120,2,32,70,1]{4,3,2,0,5,1:T(8,128)(2,1)} %copy.91, bf16[2,4,120,70,1,1]{3,2,1,0,5,4:T(8,128)(2,1)S(1)} %bitcast.78), kind=kOutput, calls=%fused_computation.2 | convolution fusion | flops 206438400 | bytes 31837440 | tf_op jit(solution)/shard_map/ijcrp,dvjp->ijcdrv/dot_general | solution.py:16
  201.7 10.6 %fusion.8 = (bf16[24,120,1,32,4]{3,4,0,1,2:T(4,128)(2,1)S(1)}, bf16[24,120,1,32,4]{3,4,0,1,2:T(4,128)(2,1)S(1)}) fusion(f32[24,120,2,2,32,4]{4,5,2,0,3,1:T(4,128)} %convolution_bitcast_fusion, f32[24,120,32]{2,0,1:T(8,128)S(1)} %fusion.11), kind=kLoop, calls=%fused_computation.11 | loop fusion | flops 2211840 | bytes 7741440 | tf_op jit(solution)/shard_map/convert
  212.3 7.4 %maximum_bitcast_fusion = bf16[24,120,2,32,4,1]{3,4,0,1,2,5:T(4,128)(2,1)} fusion(bf16[24,120,1,32,4]{3,4,0,1,2:T(4,128)(2,1)S(1)} %get-tuple-element.6, bf16[24,120,1,32,4]{3,4,0,1,2:T(4,128)(2,1)S(1)} %get-tuple-element.5), kind=kLoop, calls=%fused_computation.13 | loop fusion | flops 737280 | bytes 2949120 | tf_op jit(solution)/shard_map/stack | solution.py:24
  219.7 8.5 %copy.92 = bf16[24,120,2,32,4,1]{1,4,3,5,2,0:T(4,128)(2,1)S(1)} copy(bf16[24,120,2,32,4,1]{3,4,0,1,2,5:T(4,128)(2,1)} %maximum_bitcast_fusion) | data formatting | bytes 2949120 | tf_op jit(solution)/shard_map/stack | solution.py:24
  228.3 14.5 %fusion.12 = f32[2,2,4,24,70]{4,2,0,1,3:T(4,128)S(1)} fusion(bf16[24,120,2,32,4,1]{1,4,3,5,2,0:T(4,128)(2,1)S(1)} %copy.92, bf16[24,120,2,32,70,1]{1,3,4,2,0,5:T(8,128)(2,1)} %bitcast.82), kind=kOutput, calls=%fused_computation.19 | convolution fusion | flops 206438400 | bytes 27386880 | tf_op jit(solution)/shard_map/ijcrq,ijdrm->cdmiq/dot_general | solution.py:26
  242.8 0.1 add.86
  242.9 0.1 sub.29
  243.1 30.7 %all-gather = bf16[16,4,1680]{2,1,0:T(4,128)(2,1)S(1)} all-gather(bf16[2,4,1680]{2,1,0:T(4,128)(2,1)S(1)} %pad_maximum_fusion), channel_id=2, replica_groups=mesh['freq'=4,'tile'=8] {'tile'}, dimensions={0}, use_global_device_ids=true | all-gather | bytes 241920 | tf_op jit(solution)/shard_map/all_gather | solution.py:53
  273.8 9.3 %all_gather.7 = bf16[32,2,4,1680]{3,2,1,0:T(4,128)(2,1)S(1)} all-gather(bf16[8,2,4,1680]{3,2,1,0:T(4,128)(2,1)S(1)} %bitcast.80), channel_id=1, replica_groups=mesh['freq'=4,'tile'=8] {'freq'}, dimensions={0}, use_global_device_ids=true | all-gather | bytes 1075200 | tf_op jit(solution)/shard_map/all_gather | solution.py:54
  283.1 1.5 fusion.10
  284.5 0.1 copy.88
  284.7 1.4 convert_element_type.60
  (6 shorter events, 0.1 us)
Async XLA Ops:
  6.5 83.6 %all-reduce.4.cloned.1.call-start = ((), (), s32[]{:S(2)}) async-start(), calls=%async_computation | async-start | bytes 2162688
  12.3 76.6 %copy-start = (s32[1,24,120]{2,1,0:T(8,128)S(1)}, s32[1,24,120]{2,1,0:T(8,128)}, u32[]{:S(2)}) copy-start(s32[1,24,120]{2,1,0:T(8,128)} %param.9) | copy-start | bytes 34564
  12.3 76.6 %copy-start.2 = (u32[32]{0:T(128)S(1)}, u32[32]{0:T(128)}, u32[]{:S(2)}) copy-start(u32[32]{0:T(128)} %constant.49) | copy-start | bytes 388
  12.3 77.2 %copy-start.1 = (s32[4]{0:T(128)S(1)}, s32[4]{0:T(128)}, u32[]{:S(2)}) copy-start(s32[4]{0:T(128)} %param.10) | copy-start | bytes 52
Sparse Core Ops, SparseCore 0:
  12.4 39.0 all-reduce.3
where the time goes:
time: 293 us
  local copies, waits for them, and re-layouts  91.9 us (31%)
  matrix products  85 us (29%)
  blocking collectives  82.3 us (28%)
  other arithmetic  19.4 us (7%)
  between operations  14.2 us (5%)
    squeeze x1, local copies, waits for them, and re-layouts, local(): received = apply_kernel(v_bases[0], u_bases[0], ranks[0], frequency_spectra)  76.5 us
    dot_general x1, matrix products, apply_kernel(): jnp.einsum('ijcrp,dvjp->ijcdrv', v_part, frequency_spectra, preferred_ele...  67.3 us
    psum x1, blocking collectives, local(): frequency_spectra = lax.psum(grouped, 'tile').astype(jnp.bfloat16)  42.3 us
    all_gather x1, blocking collectives, local(): grouped_rows = lax.all_gather(piece, 'tile', axis=0, tiled=True)  30.7 us
    dot_general x1, matrix products, apply_kernel(): jnp.einsum('ijcrq,ijdrm->cdmiq', u_part, coefs, preferred_element_type=jn...  14.5 us
    another operation x1, other arithmetic  10.6 us
    all_gather x1, blocking collectives, local(): lax.all_gather(grouped_rows.astype(jnp.bfloat16), 'freq', axis=0, tiled=T...  9.31 us
    another operation x1, local copies, waits for them, and re-layouts, apply_kernel(): jnp.stack([coef_re * rank_mask, coef_im * rank_mask], axis=2)  8.54 us
  transfers between devices with their start and end apart: 1, of which 0 were waited for; matrix products, arithmetic and copies ran while one was open for 27% of the time, Pallas kernels for 0%

commit v1 on v0

v1 whole, which is shorter than its diff:
```python
import functools
import math

import jax
import jax.numpy as jnp
from jax import lax
from jax.experimental import pallas as pl
from jax.experimental.pallas import tpu as pltpu
from jax.sharding import PartitionSpec as P

LANES = 128
PACK = 16
WAYS = 2


def round_up(value, step):
    return -(-value // step) * step


def step_of(count, most, multiple=1):
    return max(k for k in range(1, most + 1) if count % k == 0 and (k * multiple) % 8 == 0)


def fold(parts, piece, size):
    return jnp.concatenate([part[..., piece * size : (piece + 1) * size] for part in parts], axis=-1)


def right_kernel(shape, x_ref, rank_ref, v_ref, out_ref, xj, xp, xg, left, right, acc):
    sources, n_group, per_group, width, ways = shape
    count, _, block, ranks, columns = v_ref.shape
    step = pl.program_id(0)
    nv = 2 * sources
    size = LANES // ways
    parts = block // ways
    lane = lax.broadcasted_iota(jnp.int32, (size, LANES), 1) % size
    diagonal = lane == lax.broadcasted_iota(jnp.int32, (size, LANES), 0)

    @pl.when(step == 0)
    def _():
        xj[...] = jnp.zeros_like(xj)
        for g in range(n_group):
            for k in range(per_group):
                j = g * per_group + k
                if j < columns:
                    xj[j * nv : (j + 1) * nv, :width] = x_ref[g, :, k * width : (k + 1) * width]
        for v in range(nv):
            xp[v] = xj[pl.ds(v, LANES, nv), :].T
            rows = [xp[v, pl.ds(a, width // ways, ways), :] for a in range(ways)]
            for g in range(ways):
                xg[g, v] = fold(rows, g, size)

    blank = jnp.zeros((count * ranks, LANES - columns), jnp.bfloat16)
    for q in range(parts):
        for c in range(2):
            rows = [
                jnp.concatenate([v_ref[:, c, q * ways + a].reshape(count * ranks, columns), blank], axis=1)
                for a in range(ways)
            ]
            at = (q * 2 + c) * LANES
            for g in range(ways):
                left[g, :, at : at + LANES] = fold(rows, g, size)
                for v in range(nv):
                    take = v if c == 0 else (v + sources) % nv
                    row = xg[g, take, pl.ds(step * parts + q, 1), :]
                    if c == 1 and v < sources:
                        row = -row
                    right[g, v * size : (v + 1) * size, at : at + LANES] = jnp.where(
                        diagonal, row, 0.0
                    ).astype(jnp.bfloat16)
    for g in range(ways):
        product = lax.dot_general(
            left[g], right[g], (((1,), (1,)), ((), ())), preferred_element_type=jnp.float32
        )

        @pl.when(step == 0)
        def _():
            acc[g] = product

        @pl.when(step > 0)
        def _():
            acc[g] += product

    @pl.when(step == pl.num_programs(0) - 1)
    def _():
        @pl.loop(0, count)
        def _(i):
            rank = rank_ref[i]
            for h in range(ranks // PACK):
                first = pl.multiple_of(i * ranks + h * PACK, PACK)
                live = lax.broadcasted_iota(jnp.int32, (PACK, LANES), 0) + h * PACK < rank
                for v in range(nv):
                    pieces = [acc[g, pl.ds(first, PACK), v * size : (v + 1) * size] for g in range(ways)]
                    coef = jnp.where(live, jnp.concatenate(pieces, axis=1), 0.0)
                    out_ref[i, h, v * PACK : (v + 1) * PACK, :LANES] = coef.astype(jnp.bfloat16)
                    other = (v + sources) % nv
                    signed = -coef if v >= sources else coef
                    out_ref[i, h, other * PACK : (other + 1) * PACK, LANES:] = signed.astype(jnp.bfloat16)


def left_kernel(nv, u_ref, b_ref, out_ref, total):
    count, _, width, ranks, columns = u_ref.shape
    step = pl.program_id(0)
    lane = lax.broadcasted_iota(jnp.int32, (1, 8, nv * PACK), 2) % PACK
    lower = lane < 8
    keep = lane % 8 == lax.broadcasted_iota(jnp.int32, (1, 8, nv * PACK), 1)
    blank = jnp.zeros((width * PACK, LANES - columns), jnp.bfloat16)
    sums = []
    for i in range(count):
        kept = None
        for h in range(ranks // PACK):
            rows = []
            for c in range(2):
                rows.append(u_ref[i, c, :, h * PACK : (h + 1) * PACK].reshape(width * PACK, columns))
                rows.append(blank)
            grid = lax.dot_general(
                jnp.concatenate(rows, axis=1),
                b_ref[i, h],
                (((1,), (1,)), ((), ())),
                preferred_element_type=jnp.float32,
            ).reshape(width, 2, 8, nv * PACK)
            part = jnp.where(lower, grid[:, 0], grid[:, 1])
            kept = part if kept is None else kept + part
        sums.append(jnp.sum(jnp.where(keep, kept, 0.0), axis=1))
    rows = count * width
    total[pl.ds(pl.multiple_of(step * rows, 8), rows), :] = jnp.concatenate(sums, axis=0).astype(total.dtype)

    @pl.when(step == pl.num_programs(0) - 1)
    def _():
        lanes = lax.broadcasted_iota(jnp.int32, (nv, nv * PACK), 1)
        part = lax.broadcasted_iota(jnp.int32, (nv, nv * PACK), 0)
        pick = (lanes // PACK == part).astype(jnp.float32)
        out_ref[...] = lax.dot_general(
            pick,
            total[...],
            (((1,), (1,)), ((), ())),
            precision=lax.Precision.HIGHEST,
            preferred_element_type=jnp.float32,
        ).astype(jnp.bfloat16)


def tile_product(v_bases, u_bases, ranks, x):
    count, _, width, depth, columns = v_bases.shape
    n_group, nv, _ = x.shape
    sources = nv // 2
    per_group = -(-columns // n_group)
    halves = depth // PACK
    ways = WAYS
    size = LANES // ways
    block = max(k for k in range(ways, 11, ways) if width % k == 0)
    rank_rows = jnp.pad(ranks, ((0, 0), (0, LANES - columns)))[:, None, :]
    coefs = pl.pallas_call(
        functools.partial(right_kernel, (sources, n_group, per_group, width, ways)),
        grid=(width // block,),
        in_specs=[
            pl.BlockSpec(x.shape, lambda s: (0, 0, 0)),
            pl.BlockSpec(rank_rows.shape, lambda s: (0, 0, 0)),
            pl.BlockSpec((count, 2, block, depth, columns), lambda s: (0, 0, s, 0, 0)),
        ],
        out_specs=pl.BlockSpec((count, halves, nv * PACK, 2 * LANES), lambda s: (0, 0, 0, 0)),
        out_shape=jax.ShapeDtypeStruct((count, halves, nv * PACK, 2 * LANES), jnp.bfloat16),
        scratch_shapes=[
            pltpu.VMEM((LANES * nv, LANES), jnp.float32),
            pltpu.VMEM((nv, LANES, LANES), jnp.float32),
            pltpu.VMEM((ways, nv, width // ways, LANES), jnp.float32),
            pltpu.VMEM((ways, count * depth, block // ways * 2 * LANES), jnp.bfloat16),
            pltpu.VMEM((ways, nv * size, block // ways * 2 * LANES), jnp.bfloat16),
            pltpu.VMEM((ways, count * depth, nv * size), jnp.float32),
        ],
        compiler_params=pltpu.CompilerParams(vmem_limit_bytes=48 * 1024 * 1024),
        cost_estimate=pl.CostEstimate(
            flops=4 * v_bases.size * nv, bytes_accessed=2 * v_bases.size, transcendentals=0
        ),
    )(x, rank_rows, v_bases)
    group = step_of(count, 4, width)
    return pl.pallas_call(
        functools.partial(left_kernel, nv),
        grid=(count // group,),
        in_specs=[
            pl.BlockSpec((group, 2, width, depth, columns), lambda s: (s, 0, 0, 0, 0)),
            pl.BlockSpec((group, halves, nv * PACK, 2 * LANES), lambda s: (s, 0, 0, 0)),
        ],
        out_specs=pl.BlockSpec((nv, count * width), lambda s: (0, 0)),
        out_shape=jax.ShapeDtypeStruct((nv, count * width), jnp.bfloat16),
        scratch_shapes=[pltpu.VMEM((count * width, nv * PACK), jnp.float32)],
        compiler_params=pltpu.CompilerParams(vmem_limit_bytes=48 * 1024 * 1024),
        cost_estimate=pl.CostEstimate(
            flops=4 * u_bases.size * nv, bytes_accessed=2 * u_bases.size, transcendentals=0
        ),
    )(u_bases, coefs)


def angles_of(freq_bin, times, total):
    products = freq_bin[:, None] * times[None, :] % total
    return products.astype(jnp.float32) * (2.0 * math.pi / total)


def gather_all(piece, axis):
    count = lax.axis_size(axis)
    me = lax.axis_index(axis)
    pieces, owners = [piece], [me]
    for s in range(1, count):
        if count & (count - 1) == 0:
            perm = [(d, d ^ s) for d in range(count)]
            owners.append(me ^ s)
        else:
            perm = [(d, (d + s) % count) for d in range(count)]
            owners.append((me - s) % count)
        pieces.append(lax.ppermute(piece, axis, perm))
    return jnp.stack(pieces), jnp.stack(owners)


def local(virtual_source_trace, v_bases, u_bases, ranks, freq_bin, slab_order):
    n_tile = lax.axis_size("tile")
    n_freq = lax.axis_size("freq")
    devices = n_freq * n_tile
    steps_dev, sources, _ = virtual_source_trace.shape
    total = steps_dev * devices
    columns = v_bases.shape[2]
    width = v_bases.shape[5]
    rows_dev = v_bases.shape[1] * width
    both = ("freq", "tile")

    n_group = devices // sources
    per_group = -(-columns // n_group)
    lanes = round_up(per_group * width, LANES)
    raw = virtual_source_trace.reshape(steps_dev, sources, columns * width)
    raw = jnp.pad(raw, ((0, 0), (0, 0), (0, (n_group * per_group - columns) * width)))
    raw = raw.reshape(steps_dev, sources, n_group, per_group * width)
    raw = jnp.pad(raw, ((0, 0), (0, 0), (0, 0), (0, lanes - per_group * width)))
    raw = raw.transpose(1, 2, 0, 3).reshape(devices, steps_dev, lanes)
    raw = lax.all_to_all(raw, both, 0, 0, tiled=True).reshape(total, lanes)

    times = (slab_order[:, None] * steps_dev + jnp.arange(steps_dev, dtype=jnp.int32)[None, :]).reshape(total)
    angles = angles_of(freq_bin, times, total)
    forward = jnp.stack([jnp.cos(angles), -jnp.sin(angles)], axis=1) / math.sqrt(total)
    spectra = jnp.einsum("fct,tl->fcl", forward, raw.astype(jnp.float32), precision=lax.Precision.HIGHEST)
    spectra = spectra.astype(jnp.bfloat16)
    spectra = jnp.broadcast_to(spectra[:, None], (n_freq, n_tile, 2, lanes)).reshape(devices, 2, lanes)
    spectra = lax.all_to_all(spectra, both, 0, 0, tiled=True)
    spectra = spectra.reshape(sources, n_group, 2, lanes).transpose(1, 2, 0, 3)
    spectra = spectra.reshape(n_group, 2 * sources, lanes).astype(jnp.float32)

    order = (0, 2, 4, 3, 1)
    received = tile_product(v_bases[0].transpose(order), u_bases[0].transpose(order), ranks[0], spectra)

    gathered, owners = gather_all(received, "freq")
    gathered = gathered.reshape(n_freq, 2, sources, rows_dev).astype(jnp.float32)
    group = lax.dynamic_slice_in_dim(slab_order, lax.axis_index("freq") * n_tile, n_tile)
    times = (group[:, None] * steps_dev + jnp.arange(steps_dev, dtype=jnp.int32)[None, :]).reshape(-1)
    angles = angles_of(freq_bin[owners], times, total).T
    inverse = jnp.stack([jnp.cos(angles), -jnp.sin(angles)], axis=2) / math.sqrt(freq_bin.shape[0])
    wave = jnp.einsum("tgc,gcvn->tvn", inverse, gathered, precision=lax.Precision.HIGHEST)
    wave = wave.astype(jnp.bfloat16).reshape(n_tile, steps_dev, sources, rows_dev)
    wave = lax.all_to_all(wave, "tile", 0, 0, tiled=True)
    return wave.transpose(1, 2, 0, 3).reshape(steps_dev, sources, n_tile * rows_dev)


def solution(mesh):
    in_specs = (
        P(("freq", "tile"), None, None),
        P("freq", "tile", None, None, None, None),
        P("freq", "tile", None, None, None, None),
        P("freq", "tile", None),
        P(),
        P(),
    )
    out_specs = P(("freq", "tile"), None, None)
    return jax.shard_map(local, mesh=mesh, in_specs=in_specs, out_specs=out_specs, check_vma=False)
```

time: 293 us -> 96.6 us (0.33)
  local copies, waits for them, and re-layouts: 91.9 us -> 7.35 us
  matrix products: 85 us -> 1.09 us
  blocking collectives: 82.3 us -> 16.2 us
  Pallas kernels: 0 us -> 39.8 us
  waiting for transfers between devices: 0.04 us -> 17.1 us
  other arithmetic: 19.4 us -> 2.53 us
  between operations: 14.2 us -> 0.16 us
  starting transfers between devices: 0.01 us -> 11.8 us
    dot_general x4 -> x2, matrix products: 85 us -> 1.09 us  [the longest x1 0.84 us: local(): jnp.einsum('tgc,gcvn->tvn', inverse, gathered, precision=lax.Precision.HI...]
    squeeze x1 -> x0, local copies, waits for them, and re-layouts: 76.5 us -> none  [local(): received = apply_kernel(v_bases[0], u_bases[0], ranks[0], frequency_spectra)]
    psum x1 -> x0, blocking collectives: 42.3 us -> none  [local(): frequency_spectra = lax.psum(grouped, 'tile').astype(jnp.bfloat16)]
    all_gather x2 -> x0, blocking collectives: 40 us -> none  [the longest x1 30.7 us: local(): grouped_rows = lax.all_gather(piece, 'tile', axis=0, tiled=True)]
    pallas_call x0 -> x2, Pallas kernels: none -> 39.8 us  [the longest x1 26.1 us: tile_product(): pl.pallas_call(functools.partial(right_kernel, (sources, n_group, per_gro...]
    another operation x3 -> x0, other arithmetic: 18.1 us -> none
    all_to_all x0 -> x1, blocking collectives: none -> 16.2 us  [local(): wave = lax.all_to_all(wave, 'tile', 0, 0, tiled=True)]
    all_to_all x0 -> x2, waiting for transfers between devices: none -> 14.7 us  [the longest x1 9.08 us: local(): raw = lax.all_to_all(raw, both, 0, 0, tiled=True).reshape(total, lanes)]
  transfers between devices with their start and end apart: 1 -> 5, of which waited for: 0 -> 4; matrix products, arithmetic and copies ran while one was open for 27% -> 5% of each run, Pallas kernels for 0% -> 0%
where the time goes in v1:
time: 96.6 us; the launch traced here: 96.1 us
  Pallas kernels  39.8 us (41%)
  waiting for transfers between devices  17.1 us (18%)
  blocking collectives  16.2 us (17%)
  starting transfers between devices  11.8 us (12%)
  local copies, waits for them, and re-layouts  7.35 us (8%)
  other arithmetic  2.53 us (3%)
  matrix products  1.09 us (1%)
    pallas_call x1, Pallas kernels, tile_product(): pl.pallas_call(functools.partial(right_kernel, (sources, n_group, per_gro...  26.1 us
    all_to_all x1, blocking collectives, local(): wave = lax.all_to_all(wave, 'tile', 0, 0, tiled=True)  16.2 us
    pallas_call x1, Pallas kernels, tile_product(): pl.pallas_call(functools.partial(left_kernel, nv), grid=(count // group,)...  13.7 us
    all_to_all x1, waiting for transfers between devices, local(): raw = lax.all_to_all(raw, both, 0, 0, tiled=True).reshape(total, lanes)  9.08 us
    all_to_all x1, starting transfers between devices, local(): raw = lax.all_to_all(raw, both, 0, 0, tiled=True).reshape(total, lanes)  7.3 us
    all_to_all x1, waiting for transfers between devices, local(): spectra = lax.all_to_all(spectra, both, 0, 0, tiled=True)  5.58 us
    all_to_all x1, starting transfers between devices, local(): spectra = lax.all_to_all(spectra, both, 0, 0, tiled=True)  2.58 us
    ppermute x3, waiting for transfers between devices, gather_all(): pieces.append(lax.ppermute(piece, axis, perm))  2.48 us
  transfers between devices with their start and end apart: 5, of which 4 were waited for; matrix products, arithmetic and copies ran while one was open for 5% of the time, Pallas kernels for 0%

profile of v1, /device:TPU:0, one launch (start us, length us, event | category | flops | bytes accessed | tf_op | source)
XLA Modules:
  0.0 96.1 jit_solution(11257741127918578600)
XLA Ops:
  0.0 1.3 %reshape.475 = bf16[4,4,8,1050]{3,2,1,0:T(8,128)(2,1)S(1)} reshape(bf16[4,4,8400]{2,1,0:T(4,128)(2,1)} %param.6) | data formatting | bytes 537600 | tf_op jit(solution)/shard_map/reshape | solution.py:228
  1.4 0.9 copy.30
  2.2 7.3 %all-to-all-start = ((bf16[32,4,1152]{2,1,0:T(4,128)(2,1)}), bf16[32,4,1152]{2,1,0:T(4,128)(2,1)S(1)}, u32[]{:S(2)}, u32[]{:S(2)}) async-start(bf16[32,4,1152]{2,1,0:T(4,128)(2,1)} %bitcast.9), calls=%async_computation | async-start | bytes 589824 | tf_op jit(solution)/shard_map/all_to_all | solution.py:231
  9.6 0.7 broadcast_multiply_fusion
  10.2 0.1 iota_add_fusion
  10.3 0.1 add.102
  10.4 0.7 dynamic-slice_multiply_fusion
  11.1 0.8 fusion.22
  11.9 9.1 %all-to-all-done = bf16[32,4,1152]{2,1,0:T(4,128)(2,1)S(1)} async-done(((bf16[32,4,1152]{2,1,0:T(4,128)(2,1)}), bf16[32,4,1152]{2,1,0:T(4,128)(2,1)S(1)}, u32[]{:S(2)}, u32[]{:S(2)}) %all-to-all-start) | async-done | bytes 294944 | tf_op jit(solution)/shard_map/all_to_all | solution.py:231
  21.0 0.1 reshape.491
  21.1 0.2 convolution_convert_fusion
  21.3 0.7 broadcast_in_dim.4
  22.1 2.6 %all-to-all-start.1 = ((bf16[32,2,1152]{2,1,0:T(2,128)(2,1)}), bf16[32,2,1152]{2,1,0:T(2,128)(2,1)S(1)}, u32[]{:S(2)}, u32[]{:S(2)}) async-start(bf16[32,2,1152]{2,1,0:T(2,128)(2,1)} %bitcast.10), calls=%async_computation.1 | async-start | bytes 294912 | tf_op jit(solution)/shard_map/all_to_all | solution.py:239
  24.7 0.7 pad.9
  25.5 0.1 add.97
  25.5 0.1 fusion.24
  25.6 1.3 %gather_fusion = s32[4]{0:T(128)S(1)} fusion(s32[4]{0:T(128)} %param.10, s32[1024]{0:T(1024)S(1)} %pad_clamp_fusion), kind=kCustom, calls=%fused_computation | custom fusion | bytes 48 | tf_op jit(solution)/shard_map/gather | solution.py:250
  26.9 5.6 %all-to-all-done.1 = bf16[32,2,1152]{2,1,0:T(2,128)(2,1)S(1)} async-done(((bf16[32,2,1152]{2,1,0:T(2,128)(2,1)}), bf16[32,2,1152]{2,1,0:T(2,128)(2,1)S(1)}, u32[]{:S(2)}, u32[]{:S(2)}) %all-to-all-start.1) | async-done | bytes 147488 | tf_op jit(solution)/shard_map/all_to_all | solution.py:239
  32.6 26.1 %shard_map.64.b_ref = bf16[24,2,128,256]{3,2,1,0:T(8,128)(2,1)S(1)} custom-call(f32[8,8,1152]{2,1,0:T(8,128)S(1)} %copy.41.x_ref, s32[24,1,128]{2,1,0:T(1,128)S(1)} %bitcast.38, bf16[24,2,70,32,120]{4,3,2,1,0:T(8,128)(2,1)} %bitcast.39), custom_call_target="tpu_custom_call" | custom-call | flops 412876800 | bytes 25804800 | tf_op jit(solution)/shard_map/pallas_call | solution.py:151
  58.7 13.7 %shard_map.65 = bf16[8,1680]{1,0:T(8,128)(2,1)S(1)} custom-call(bf16[24,2,70,32,120]{4,3,2,1,0:T(8,128)(2,1)} %bitcast.40, bf16[24,2,128,256]{3,2,1,0:T(8,128)(2,1)S(1)} %shard_map.64.b_ref), custom_call_target="tpu_custom_call" | custom-call | flops 412876800 | bytes 25804800 | tf_op jit(solution)/shard_map/pallas_call | solution.py:175
  72.4 0.8 collective-permute-start.2
  73.2 1.0 %collective-permute-start.1 = (bf16[8,1680]{1,0:T(8,128)(2,1)S(1)}, bf16[8,1680]{1,0:T(8,128)(2,1)S(1)}, u32[]{:S(2)}, u32[]{:S(2)}) collective-permute-start(bf16[8,1680]{1,0:T(8,128)(2,1)S(1)} %shard_map.65), channel_id=1, source_target_pairs={{0,16},{8,24},{16,0},{24,8},{1,17},{9,25},{17,1},{25,9},{2,18},{10... | collective-permute-start | bytes 80648 | tf_op jit(solution)/shard_map/ppermute | solution.py:208
  74.1 0.1 collective-permute-start
  74.3 0.1 fusion.23
  74.5 1.2 %collective-permute-done.2 = bf16[8,1680]{1,0:T(8,128)(2,1)S(1)} collective-permute-done((bf16[8,1680]{1,0:T(8,128)(2,1)S(1)}, bf16[8,1680]{1,0:T(8,128)(2,1)S(1)}, u32[]{:S(2)}, u32[]{:S(2)}) %collective-permute-start.2) | collective-permute-done | bytes 26912 | tf_op jit(solution)/shard_map/ppermute | solution.py:208
  75.8 1.2 %collective-permute-done.1 = bf16[8,1680]{1,0:T(8,128)(2,1)S(1)} collective-permute-done((bf16[8,1680]{1,0:T(8,128)(2,1)S(1)}, bf16[8,1680]{1,0:T(8,128)(2,1)S(1)}, u32[]{:S(2)}, u32[]{:S(2)}) %collective-permute-start.1) | collective-permute-done | bytes 26912 | tf_op jit(solution)/shard_map/ppermute | solution.py:208
  77.2 0.8 fusion
  78.0 0.1 reshape.479
  78.2 0.2 copy.38
  78.3 16.2 %all_to_all.15 = bf16[8,4,4,1680]{3,1,2,0:T(4,128)(2,1)S(1)} all-to-all(bf16[8,4,4,1680]{3,1,2,0:T(4,128)(2,1)S(1)} %copy.38), channel_id=1, replica_groups=mesh['freq'=4,'tile'=8] {'tile'}, dimensions={0} | all-to-all | bytes 860160 | tf_op jit(solution)/shard_map/all_to_all | solution.py:254
  94.6 0.1 copy.39
  94.7 1.4 %reshape.480 = bf16[4,4,13440]{2,1,0:T(4,128)(2,1)} reshape(bf16[4,4,8,1680]{3,2,1,0:T(8,128)(2,1)S(1)} %copy.39) | data formatting | bytes 860160 | tf_op jit(solution)/shard_map/reshape | solution.py:255
  (15 shorter events, 0.5 us)
Async XLA Ops:
  2.2 18.7 %all-to-all-start = ((bf16[32,4,1152]{2,1,0:T(4,128)(2,1)}), bf16[32,4,1152]{2,1,0:T(4,128)(2,1)S(1)}, u32[]{:S(2)}, u32[]{:S(2)}) async-start(bf16[32,4,1152]{2,1,0:T(4,128)(2,1)} %bitcast.9), calls=%async_computation | async-start | bytes 589824 | tf_op jit(solution)/shard_map/all_to_all | solution.py:231
  22.1 10.4 %all-to-all-start.1 = ((bf16[32,2,1152]{2,1,0:T(2,128)(2,1)}), bf16[32,2,1152]{2,1,0:T(2,128)(2,1)S(1)}, u32[]{:S(2)}, u32[]{:S(2)}) async-start(bf16[32,2,1152]{2,1,0:T(2,128)(2,1)} %bitcast.10), calls=%async_computation.1 | async-start | bytes 294912 | tf_op jit(solution)/shard_map/all_to_all | solution.py:239
  72.4 3.3 %collective-permute-start.2 = (bf16[8,1680]{1,0:T(8,128)(2,1)S(1)}, bf16[8,1680]{1,0:T(8,128)(2,1)S(1)}, u32[]{:S(2)}, u32[]{:S(2)}) collective-permute-start(bf16[8,1680]{1,0:T(8,128)(2,1)S(1)} %shard_map.65), channel_id=1, source_target_pairs={{0,24},{8,16},{16,8},{24,0},{1,25},{9,17},{17,9},{25,1},{2,26},{10... | collective-permute-start | bytes 80648 | tf_op jit(solution)/shard_map/ppermute | solution.py:208
  73.2 3.9 %collective-permute-start.1 = (bf16[8,1680]{1,0:T(8,128)(2,1)S(1)}, bf16[8,1680]{1,0:T(8,128)(2,1)S(1)}, u32[]{:S(2)}, u32[]{:S(2)}) collective-permute-start(bf16[8,1680]{1,0:T(8,128)(2,1)S(1)} %shard_map.65), channel_id=1, source_target_pairs={{0,16},{8,24},{16,0},{24,8},{1,17},{9,25},{17,1},{25,9},{2,18},{10... | collective-permute-start | bytes 80648 | tf_op jit(solution)/shard_map/ppermute | solution.py:208
  74.1 3.0 %collective-permute-start = (bf16[8,1680]{1,0:T(8,128)(2,1)S(1)}, bf16[8,1680]{1,0:T(8,128)(2,1)S(1)}, u32[]{:S(2)}, u32[]{:S(2)}) collective-permute-start(bf16[8,1680]{1,0:T(8,128)(2,1)S(1)} %shard_map.65), channel_id=1, source_target_pairs={{0,8},{8,0},{16,24},{24,16},{1,9},{9,1},{17,25},{25,17},{2,10},{10... | collective-permute-start | bytes 80648 | tf_op jit(solution)/shard_map/ppermute | solution.py:208
